TPU v7x, 512 devices: a whole 4x8x8 slice. The times are simulated.
512 devices in a mesh: seq: 16 (over z, core), chan: 32 (over x, y).
Axes of the slice: x: 4, y: 8, z: 8, core: 2. Of those that a mesh axis runs over, the one named last changes fastest.
Arguments:
- tokens: bfloat16 [4096, 4096], P('seq', 'chan'), may hold values from -6 to 6
- w_in: bfloat16 [4096, 3, 4096], P(None, None, 'chan'), may hold values from -0.09375 to 0.09375
- filters: bfloat16 [256, 4096], P('chan'), may hold values from -0.09375 to 0.09375
- skip: float32 [4096], P('chan'), may hold values from 0.25 to 1.5
- w_out: bfloat16 [4096, 4096], P(None, 'chan'), may hold values from -0.09375 to 0.09375
Outputs:
- mixed: bfloat16 [4096, 4096], P('seq', 'chan')
All inputs are finite; a program needn't handle non-finite values.
Results may differ from a plain program's by a relative error of at most 0.015.
Values may be sent and summed in bfloat16 or wider, within the bound.
No kernel may reach another device: no remote copies, remote signals or barrier semaphores. Data moves between devices by JAX's collectives and lax.ppermute only.
A program may use at most 64 MiB of HBM per device.

v0:
```python
import math
import jax
import jax.numpy as jnp
from jax import lax
from jax.sharding import PartitionSpec as P


def toeplitz(padded, lead, offset, rows, cols):
    span = rows + cols
    segment = lax.dynamic_slice_in_dim(padded, lead + offset - cols + 1, span, 1)
    rolled = jnp.concatenate([segment[:, cols - 1 :], segment[:, : cols - 1]], axis=1)
    flat = jnp.tile(rolled, (1, cols))[:, : cols * (span - 1)]
    return flat.reshape(padded.shape[0], cols, span - 1)[:, :, :rows]


def apply_groups(matrix, values):
    groups = matrix.shape[0]
    grouped = values.reshape(values.shape[0], groups, -1)
    result = jnp.einsum("jgc,gji->gci", grouped, matrix, preferred_element_type=jnp.float32)
    return result.reshape(values.shape[1], matrix.shape[2]).T


def shards(tokens, w_in, filters, skip, w_out):
    block_len = tokens.shape[0]
    chans = w_out.shape[1]
    w_flat = w_in.reshape(w_in.shape[0], 3 * chans)
    rows = w_flat
    qkv = jnp.dot(
        lax.all_gather(tokens, "chan", axis=1, tiled=True), rows, preferred_element_type=jnp.float32
    )
    qkv = qkv.astype(jnp.bfloat16).reshape(block_len, 3, chans)
    query = qkv[:, 0]
    source = (qkv[:, 1].astype(jnp.float32) * qkv[:, 2].astype(jnp.float32)).astype(jnp.bfloat16)
    seq_rank = lax.axis_index("seq")
    lead = 2 * block_len
    row_first = seq_rank * block_len
    padded = jnp.pad(filters, ((0, 0), (lead, 1)))
    piece = lax.all_gather(source, "seq", axis=0, tiled=True)
    width = math.gcd(piece.shape[0], block_len)

    def visit(turn, carry):
        col_first = turn * width
        sub_block = lax.dynamic_slice_in_dim(piece, turn * width, width, 0)

        def contribute(acc):
            matrix = toeplitz(padded, lead, row_first - col_first, block_len, width)
            return acc + apply_groups(matrix, sub_block)

        return lax.cond(col_first < row_first + block_len, contribute, lambda acc: acc, carry)

    conv = lax.fori_loop(
        0, piece.shape[0] // width, visit, jnp.zeros((block_len, chans), jnp.float32)
    )
    gated = (
        query.astype(jnp.float32) * (conv + skip[None, :] * source.astype(jnp.float32))
    ).astype(jnp.bfloat16)
    rows = w_out
    mixed = jnp.dot(
        lax.all_gather(gated, "chan", axis=1, tiled=True), rows, preferred_element_type=jnp.float32
    )
    return mixed.astype(jnp.bfloat16)


def solution(mesh):
    in_specs = (
        P("seq", "chan"),
        P(None, None, "chan"),
        P("chan", None),
        P("chan"),
        P(None, "chan"),
    )
    out_specs = P("seq", "chan")
    return jax.shard_map(shards, mesh=mesh, in_specs=in_specs, out_specs=out_specs, check_vma=False)
```

profile of v0, /device:TPU:16, one launch (start us, length us, event | category | flops | bytes accessed | tf_op | source)
XLA Modules:
  0.0 409.9 jit_solution(13379084503499515155)
XLA Ops:
  6.5 0.0 copy-start
  6.5 0.0 all-gather.5.cloned.1.call-start
  6.5 0.7 all-gather.5.cloned.1.call-update
  7.3 0.0 all-gather.9.cloned.1.call-start
  7.3 4.7 %copy.9 = bf16[4096,3,128]{0,2,1:T(8,128)(2,1)} copy(bf16[4096,3,128]{2,0,1:T(8,128)(2,1)} %param.10) | data formatting | bytes 6291456 | tf_op args[1]
  12.0 82.4 %all-gather.5.cloned.1.call-done = bf16[256,4096]{1,0:T(8,128)(2,1)} async-done(((bf16[256,128]{1,0:T(8,128)(2,1)}), bf16[256,4096]{1,0:T(8,128)(2,1)}) %all-gather.5.cloned.1.call-update) | async-done | bytes 2097168 | tf_op jit(solution)/shard_map/all_gather | solution.py:29
  94.4 0.0 copy-start.1
  94.4 3.8 convolution_convert_fusion
  98.2 0.1 copy.10
  98.4 0.6 multiply_convert_fusion
  99.0 0.0 all-gather.9.cloned.1.call-update
  99.0 0.0 all-gather.7.cloned.1.call-start
  99.1 0.0 copy-done.1
  99.1 41.1 %all-gather.9.cloned.1.call-done = bf16[4096,1,128]{0,2,1:T(8,128)(2,1)} async-done(((bf16[256,1,128]{0,2,1:T(8,128)(2,1)}), bf16[4096,1,128]{0,2,1:T(8,128)(2,1)}) %all-gather.9.cloned.1.call-update) | async-done | bytes 1048592 | tf_op jit(solution)/shard_map/all_gather | solution.py:38
  140.2 0.0 copy-start.2
  140.2 11.8 %while.17 = (s32[]{:T(128)}, f32[256,128]{0,1:T(8,128)S(1)}, s32[]{:T(128)}, bf16[4096,128]{0,1:T(8,128)(2,1)}, s32[]{:T(128)}, /*index=5*/bf16[8,4609]{1,0:T(8,128)(2,1)S(1)}, s32[]{:T(128)}, s32[]{:T(128)}) while((s32[]{:T(128)}, f32[256,128]{0,1:T(8,128)S(1)}, s32[]{:T(128)}, bf16[4096,128]{0,1:T(8,128)(2,1)}, s32[]{:T(128)}, ...), condition=%wide.region_3.4_spmd, body=%wide.region_0.3_spmd.sunk | while | flops 16826380 | bytes 16466195 | solution.py:51
  140.3 11.2 %conditional.2 = (f32[256,128]{0,1:T(8,128)S(1)}) conditional(s32[]{:T(128)} %convert_element_type.67, f32[256,128]{0,1:T(8,128)S(1)} %get-tuple-element.249, (s32[]{:T(128)}, bf16[4096,128]{0,1:T(8,128)(2,1)}, s32[]{:T(128)}, bf16[8,4609]{1,0:T(8,128)(2,1)S(1)}, f32[256,128]{0,1:T(8,128)S(1)}) %tuple.50), branch_computations={%region_1.1_spmd, %region_2.2_spmd} | conditional | flops 16826376 | bytes 16466044 | solution.py:49
  140.3 0.1 constant_dynamic-slice_fusion
  140.4 0.1 constant_dynamic-slice_fusion.1
  140.5 0.1 pad_maximum_fusion
  140.5 0.1 tile.4
  140.7 0.1 slice.32
  140.8 4.4 %reshape.37 = bf16[1046528]{0:T(1024)(128)(2,1)} reshape(bf16[8,130816]{1,0:T(8,128)(2,1)S(1)} %slice.32) | data formatting | bytes 4186112 | tf_op jit(solution)/shard_map/while/body/eval_jaxpr/cond
  145.3 5.0 %reshape.28 = bf16[8,256,511]{2,1,0:T(8,128)(2,1)S(1)} reshape(bf16[1046528]{0:T(1024)(128)(2,1)} %reshape.37) | data formatting | bytes 4186112 | tf_op jit(solution)/shard_map/while/body/eval_jaxpr/cond/branch_1_fun/reshape | solution.py:13
  150.3 0.8 constant_dynamic-slice_fusion.2
  151.1 0.2 fusion
  152.1 0.0 copy-done.2
  152.1 0.7 fusion.4
  152.8 0.0 all-gather.7.cloned.1.call-update
  152.8 247.6 %all-gather.7.cloned.1.call-done = bf16[256,4096]{0,1:T(8,128)(2,1)} async-done(((bf16[256,128]{0,1:T(8,128)(2,1)}), bf16[256,4096]{0,1:T(8,128)(2,1)}) %all-gather.7.cloned.1.call-update) | async-done | bytes 2097168 | tf_op jit(solution)/shard_map/all_gather | solution.py:59
  400.4 0.0 copy-done
  400.4 3.0 convolution_convert_fusion.1
  (18 shorter events, 0.2 us)
Async XLA Ops:
  6.5 393.9 %copy-start = (bf16[4096,128]{1,0:T(8,128)(2,1)S(1)}, bf16[4096,128]{1,0:T(8,128)(2,1)}, u32[]{:S(2)}) copy-start(bf16[4096,128]{1,0:T(8,128)(2,1)} %param.13) | copy-start | bytes 3145732
  6.5 87.8 %all-gather.5.cloned.1.call-start = ((), (), s32[]{:S(2)}) async-start(), calls=%async_computation | async-start | bytes 2162688 | tf_op jit(solution)/shard_map/all_gather | solution.py:29
  7.3 133.0 %all-gather.9.cloned.1.call-start = ((), (), s32[]{:S(2)}) async-start(), calls=%async_computation.2 | async-start | bytes 1114112 | tf_op jit(solution)/shard_map/all_gather | solution.py:38
  94.4 4.7 %copy-start.1 = (bf16[8,4096]{1,0:T(8,128)(2,1)S(1)}, bf16[8,4096]{1,0:T(8,128)(2,1)}, u32[]{:S(2)}) copy-start(bf16[8,4096]{1,0:T(8,128)(2,1)} %param.11) | copy-start | bytes 196612
  99.0 301.4 %all-gather.7.cloned.1.call-start = ((), (), s32[]{:S(2)}) async-start(), calls=%async_computation.1 | async-start | bytes 2162688 | tf_op jit(solution)/shard_map/all_gather | solution.py:59
  140.2 11.8 %copy-start.2 = (f32[128]{0:T(128)S(1)}, f32[128]{0:T(128)}, u32[]{:S(2)}) copy-start(f32[128]{0:T(128)} %param.12) | copy-start | bytes 1540
Sparse Core Ops, SparseCore 0:
  10.4 83.9 all-gather.4
  99.1 41.0 all-gather.8
  152.9 247.4 all-gather.6
where the time goes:
time: 411 us; the launch traced here: 410 us
  waiting for transfers between devices  372 us (91%)
  local copies, waits for them, and re-layouts  15.6 us (4%)
  between operations  13.2 us (3%)
  matrix products  7.03 us (2%)
    all_gather x1, waiting for transfers between devices, shards(): lax.all_gather(gated, 'chan', axis=1, tiled=True)  248 us
    all_gather x1, waiting for transfers between devices, shards(): lax.all_gather(tokens, 'chan', axis=1, tiled=True)  82.4 us
    all_gather x1, waiting for transfers between devices, shards(): piece = lax.all_gather(source, 'seq', axis=0, tiled=True)  41.1 us
  transfers between devices with their start and end apart: 3, of which 3 were waited for; matrix products, arithmetic and copies ran while one was open for 1% of the time, Pallas kernels for 0%

commit v1 on v0

--- a/solution.py
+++ b/solution.py
@@ -3,6 +3,12 @@
 import jax.numpy as jnp
 from jax import lax
 from jax.sharding import PartitionSpec as P
+
+
+def in_order(blocks, dim):
+    blocks = jnp.moveaxis(blocks, 0, dim)
+    lengths = blocks.shape
+    return blocks.reshape(*lengths[:dim], lengths[dim] * lengths[dim + 1], *lengths[dim + 2 :])
 
 
 def toeplitz(padded, lead, offset, rows, cols):
@@ -35,7 +41,14 @@
     lead = 2 * block_len
     row_first = seq_rank * block_len
     padded = jnp.pad(filters, ((0, 0), (lead, 1)))
-    piece = lax.all_gather(source, "seq", axis=0, tiled=True)
+    size = lax.axis_size("seq")
+    right = [(i, (i + 1) % size) for i in range(size)]
+    parts = [source]
+    while len(parts) < size:
+        parts.append(lax.ppermute(parts[-1], "seq", right))
+    position = lax.axis_index("seq")
+    parts = jnp.stack(parts)[(position - jnp.arange(size)) % size]
+    piece = in_order(parts, 0)
     width = math.gcd(piece.shape[0], block_len)
 
     def visit(turn, carry):

time: 411 us -> 442 us (1.075)
  waiting for transfers between devices: 372 us -> 400 us
    ppermute x0 -> x15, waiting for transfers between devices: none -> 73.3 us  [shards(): parts.append(lax.ppermute(parts[-1], 'seq', right))]
    all_gather x1 -> x0, waiting for transfers between devices: 41.1 us -> none  [shards(): piece = lax.all_gather(source, 'seq', axis=0, tiled=True)]
  transfers between devices with their start and end apart: 3 -> 17, of which waited for: 3 -> 17; matrix products, arithmetic and copies ran while one was open for 1% -> 1% of each run, Pallas kernels for 0% -> 0%
where the time goes in v1:
time: 442 us; the launch traced here: 441 us
  waiting for transfers between devices  400 us (90%)
  local copies, waits for them, and re-layouts  18.3 us (4%)
  between operations  13.6 us (3%)
  matrix products  7 us (2%)
    all_gather x1, waiting for transfers between devices, shards(): lax.all_gather(gated, 'chan', axis=1, tiled=True)  244 us
    all_gather x1, waiting for transfers between devices, shards(): lax.all_gather(tokens, 'chan', axis=1, tiled=True)  82.3 us
    ppermute x15, waiting for transfers between devices, shards(): parts.append(lax.ppermute(parts[-1], 'seq', right))  73.3 us
  transfers between devices with their start and end apart: 17, of which 17 were waited for; matrix products, arithmetic and copies ran while one was open for 1% of the time, Pallas kernels for 0%

profile of v1, /device:TPU:16, one launch (start us, length us, event | category | flops | bytes accessed | tf_op | source)
XLA Modules:
  0.0 440.7 jit_solution(1263680142012626146)
XLA Ops:
  6.5 0.7 all-gather.3.cloned.1.call-update
  7.3 0.0 all-gather.5.cloned.1.call-start
  7.3 4.7 %copy.9 = bf16[4096,3,128]{0,2,1:T(8,128)(2,1)} copy(bf16[4096,3,128]{2,0,1:T(8,128)(2,1)} %param.10) | data formatting | bytes 6291456 | tf_op args[1]
  12.1 82.3 %all-gather.3.cloned.1.call-done = bf16[256,4096]{1,0:T(8,128)(2,1)} async-done(((bf16[256,128]{1,0:T(8,128)(2,1)}), bf16[256,4096]{1,0:T(8,128)(2,1)}) %all-gather.3.cloned.1.call-update) | async-done | bytes 2097168 | tf_op jit(solution)/shard_map/all_gather | solution.py:35
  94.4 3.8 convolution_convert_fusion
  98.2 0.1 copy.10
  98.3 0.0 collective-permute-start
  98.4 4.9 %collective-permute-done = bf16[256,128]{0,1:T(8,128)(2,1)S(1)} collective-permute-done((bf16[256,128]{0,1:T(8,128)(2,1)S(1)}, bf16[256,128]{0,1:T(8,128)(2,1)S(1)}, u32[]{:S(2)}, u32[]{:S(2)}) %collective-permute-start) | collective-permute-done | bytes 65568 | tf_op jit(solution)/shard_map/ppermute | solution.py:48
  103.3 4.9 %collective-permute-done.1 = bf16[256,128]{0,1:T(8,128)(2,1)S(1)} collective-permute-done((bf16[256,128]{0,1:T(8,128)(2,1)S(1)}, bf16[256,128]{0,1:T(8,128)(2,1)S(1)}, u32[]{:S(2)}, u32[]{:S(2)}) %collective-permute-start.1) | collective-permute-done | bytes 65568 | tf_op jit(solution)/shard_map/ppermute | solution.py:48
  108.2 0.0 collective-permute-start.2
  108.2 4.9 %collective-permute-done.2 = bf16[256,128]{0,1:T(8,128)(2,1)S(1)} collective-permute-done((bf16[256,128]{0,1:T(8,128)(2,1)S(1)}, bf16[256,128]{0,1:T(8,128)(2,1)S(1)}, u32[]{:S(2)}, u32[]{:S(2)}) %collective-permute-start.2) | collective-permute-done | bytes 65568 | tf_op jit(solution)/shard_map/ppermute | solution.py:48
  113.1 0.0 collective-permute-start.3
  113.1 4.9 %collective-permute-done.3 = bf16[256,128]{0,1:T(8,128)(2,1)S(1)} collective-permute-done((bf16[256,128]{0,1:T(8,128)(2,1)S(1)}, bf16[256,128]{0,1:T(8,128)(2,1)S(1)}, u32[]{:S(2)}, u32[]{:S(2)}) %collective-permute-start.3) | collective-permute-done | bytes 65568 | tf_op jit(solution)/shard_map/ppermute | solution.py:48
  118.0 4.9 %collective-permute-done.4 = bf16[256,128]{0,1:T(8,128)(2,1)S(1)} collective-permute-done((bf16[256,128]{0,1:T(8,128)(2,1)S(1)}, bf16[256,128]{0,1:T(8,128)(2,1)S(1)}, u32[]{:S(2)}, u32[]{:S(2)}) %collective-permute-start.4) | collective-permute-done | bytes 65568 | tf_op jit(solution)/shard_map/ppermute | solution.py:48
  122.9 0.0 collective-permute-start.5
  122.9 4.9 %collective-permute-done.5 = bf16[256,128]{0,1:T(8,128)(2,1)S(1)} collective-permute-done((bf16[256,128]{0,1:T(8,128)(2,1)S(1)}, bf16[256,128]{0,1:T(8,128)(2,1)S(1)}, u32[]{:S(2)}, u32[]{:S(2)}) %collective-permute-start.5) | collective-permute-done | bytes 65568 | tf_op jit(solution)/shard_map/ppermute | solution.py:48
  127.8 0.0 collective-permute-start.6
  127.8 4.9 %collective-permute-done.6 = bf16[256,128]{0,1:T(8,128)(2,1)S(1)} collective-permute-done((bf16[256,128]{0,1:T(8,128)(2,1)S(1)}, bf16[256,128]{0,1:T(8,128)(2,1)S(1)}, u32[]{:S(2)}, u32[]{:S(2)}) %collective-permute-start.6) | collective-permute-done | bytes 65568 | tf_op jit(solution)/shard_map/ppermute | solution.py:48
  132.7 0.0 collective-permute-start.7
  132.7 4.9 %collective-permute-done.7 = bf16[256,128]{0,1:T(8,128)(2,1)S(1)} collective-permute-done((bf16[256,128]{0,1:T(8,128)(2,1)S(1)}, bf16[256,128]{0,1:T(8,128)(2,1)S(1)}, u32[]{:S(2)}, u32[]{:S(2)}) %collective-permute-start.7) | collective-permute-done | bytes 65568 | tf_op jit(solution)/shard_map/ppermute | solution.py:48
  137.6 4.9 %collective-permute-done.8 = bf16[256,128]{0,1:T(8,128)(2,1)S(1)} collective-permute-done((bf16[256,128]{0,1:T(8,128)(2,1)S(1)}, bf16[256,128]{0,1:T(8,128)(2,1)S(1)}, u32[]{:S(2)}, u32[]{:S(2)}) %collective-permute-start.8) | collective-permute-done | bytes 65568 | tf_op jit(solution)/shard_map/ppermute | solution.py:48
  142.5 0.0 collective-permute-start.9
  142.5 4.9 %collective-permute-done.9 = bf16[256,128]{0,1:T(8,128)(2,1)S(1)} collective-permute-done((bf16[256,128]{0,1:T(8,128)(2,1)S(1)}, bf16[256,128]{0,1:T(8,128)(2,1)S(1)}, u32[]{:S(2)}, u32[]{:S(2)}) %collective-permute-start.9) | collective-permute-done | bytes 65568 | tf_op jit(solution)/shard_map/ppermute | solution.py:48
  147.4 0.0 collective-permute-start.10
  147.4 4.9 %collective-permute-done.10 = bf16[256,128]{0,1:T(8,128)(2,1)S(1)} collective-permute-done((bf16[256,128]{0,1:T(8,128)(2,1)S(1)}, bf16[256,128]{0,1:T(8,128)(2,1)S(1)}, u32[]{:S(2)}, u32[]{:S(2)}) %collective-permute-start.10) | collective-permute-done | bytes 65568 | tf_op jit(solution)/shard_map/ppermute | solution.py:48
  152.3 4.9 %collective-permute-done.11 = bf16[256,128]{0,1:T(8,128)(2,1)S(1)} collective-permute-done((bf16[256,128]{0,1:T(8,128)(2,1)S(1)}, bf16[256,128]{0,1:T(8,128)(2,1)S(1)}, u32[]{:S(2)}, u32[]{:S(2)}) %collective-permute-start.11) | collective-permute-done | bytes 65568 | tf_op jit(solution)/shard_map/ppermute | solution.py:48
  157.2 4.9 %collective-permute-done.12 = bf16[256,128]{0,1:T(8,128)(2,1)S(1)} collective-permute-done((bf16[256,128]{0,1:T(8,128)(2,1)S(1)}, bf16[256,128]{0,1:T(8,128)(2,1)S(1)}, u32[]{:S(2)}, u32[]{:S(2)}) %collective-permute-start.12) | collective-permute-done | bytes 65568 | tf_op jit(solution)/shard_map/ppermute | solution.py:48
  162.1 4.9 %collective-permute-done.13 = bf16[256,128]{0,1:T(8,128)(2,1)S(1)} collective-permute-done((bf16[256,128]{0,1:T(8,128)(2,1)S(1)}, bf16[256,128]{0,1:T(8,128)(2,1)S(1)}, u32[]{:S(2)}, u32[]{:S(2)}) %collective-permute-start.13) | collective-permute-done | bytes 65568 | tf_op jit(solution)/shard_map/ppermute | solution.py:48
  167.0 4.9 %collective-permute-done.14 = bf16[256,128]{0,1:T(8,128)(2,1)S(1)} collective-permute-done((bf16[256,128]{0,1:T(8,128)(2,1)S(1)}, bf16[256,128]{0,1:T(8,128)(2,1)S(1)}, u32[]{:S(2)}, u32[]{:S(2)}) %collective-permute-start.14) | collective-permute-done | bytes 65568 | tf_op jit(solution)/shard_map/ppermute | solution.py:48
  171.9 0.6 gather_fusion
  172.5 0.7 copy.11
  173.2 1.4 copy.12
  174.6 0.0 copy-start.2
  174.6 11.8 %while.17 = (s32[]{:T(128)}, f32[256,128]{0,1:T(8,128)S(1)}, s32[]{:T(128)}, bf16[4096,128]{0,1:T(8,128)(2,1)}, s32[]{:T(128)}, /*index=5*/bf16[8,4609]{1,0:T(8,128)(2,1)S(1)}, s32[]{:T(128)}, s32[]{:T(128)}) while((s32[]{:T(128)}, f32[256,128]{0,1:T(8,128)S(1)}, s32[]{:T(128)}, bf16[4096,128]{0,1:T(8,128)(2,1)}, s32[]{:T(128)}, ...), condition=%wide.region_3.4_spmd, body=%wide.region_0.3_spmd.sunk | while | flops 16826380 | bytes 16466195 | solution.py:64
  174.6 11.2 %conditional.2 = (f32[256,128]{0,1:T(8,128)S(1)}) conditional(s32[]{:T(128)} %convert_element_type.106, f32[256,128]{0,1:T(8,128)S(1)} %get-tuple-element.255, (s32[]{:T(128)}, bf16[4096,128]{0,1:T(8,128)(2,1)}, s32[]{:T(128)}, bf16[8,4609]{1,0:T(8,128)(2,1)S(1)}, f32[256,128]{0,1:T(8,128)S(1)}) %tuple.51), branch_computations={%region_1.1_spmd, %region_2.2_spmd} | conditional | flops 16826376 | bytes 16466044 | solution.py:62
  174.6 0.1 constant_dynamic-slice_fusion
  174.7 0.1 constant_dynamic-slice_fusion.1
  174.8 0.1 pad_maximum_fusion
  174.9 0.1 tile.4
  175.0 0.1 slice.34
  175.1 4.5 %reshape.126 = bf16[1046528]{0:T(1024)(128)(2,1)} reshape(bf16[8,130816]{1,0:T(8,128)(2,1)S(1)} %slice.34) | data formatting | bytes 4186112 | tf_op jit(solution)/shard_map/while/body/eval_jaxpr/cond
  179.6 5.0 %reshape.109 = bf16[8,256,511]{2,1,0:T(8,128)(2,1)S(1)} reshape(bf16[1046528]{0:T(1024)(128)(2,1)} %reshape.126) | data formatting | bytes 4186112 | tf_op jit(solution)/shard_map/while/body/eval_jaxpr/cond/branch_1_fun/reshape | solution.py:19
  184.6 0.8 constant_dynamic-slice_fusion.2
  185.5 0.2 fusion
  186.4 0.7 fusion.2
  187.1 0.0 all-gather.5.cloned.1.call-update
  187.1 243.8 %all-gather.5.cloned.1.call-done = bf16[256,4096]{0,1:T(8,128)(2,1)} async-done(((bf16[256,128]{0,1:T(8,128)(2,1)}), bf16[256,4096]{0,1:T(8,128)(2,1)}) %all-gather.5.cloned.1.call-update) | async-done | bytes 2097168 | tf_op jit(solution)/shard_map/all_gather | solution.py:72
  430.9 3.0 convolution_convert_fusion.1
  (50 shorter events, 0.4 us)
Async XLA Ops:
  6.5 424.4 %copy-start = (bf16[4096,128]{1,0:T(8,128)(2,1)S(1)}, bf16[4096,128]{1,0:T(8,128)(2,1)}, u32[]{:S(2)}) copy-start(bf16[4096,128]{1,0:T(8,128)(2,1)} %param.13) | copy-start | bytes 3145732
  6.5 87.8 %all-gather.3.cloned.1.call-start = ((), (), s32[]{:S(2)}) async-start(), calls=%async_computation | async-start | bytes 2162688 | tf_op jit(solution)/shard_map/all_gather | solution.py:35
  7.3 423.6 %all-gather.5.cloned.1.call-start = ((), (), s32[]{:S(2)}) async-start(), calls=%async_computation.1 | async-start | bytes 2162688 | tf_op jit(solution)/shard_map/all_gather | solution.py:72
  7.3 4.7 %copy-start.1 = (bf16[8,4096]{1,0:T(8,128)(2,1)S(1)}, bf16[8,4096]{1,0:T(8,128)(2,1)}, u32[]{:S(2)}) copy-start(bf16[8,4096]{1,0:T(8,128)(2,1)} %param.11) | copy-start | bytes 196612
  98.3 4.9 %collective-permute-start = (bf16[256,128]{0,1:T(8,128)(2,1)S(1)}, bf16[256,128]{0,1:T(8,128)(2,1)S(1)}, u32[]{:S(2)}, u32[]{:S(2)}) collective-permute-start(bf16[256,128]{0,1:T(8,128)(2,1)S(1)} %fusion.3), channel_id=1, source_target_pairs={{0,32},{32,64},{64,96},{96,128},{128,160},{160,192},{192,224},{224... | collective-permute-start | bytes 196616 | tf_op jit(solution)/shard_map/ppermute | solution.py:48
  103.3 4.9 %collective-permute-start.1 = (bf16[256,128]{0,1:T(8,128)(2,1)S(1)}, bf16[256,128]{0,1:T(8,128)(2,1)S(1)}, u32[]{:S(2)}, u32[]{:S(2)}) collective-permute-start(bf16[256,128]{0,1:T(8,128)(2,1)S(1)} %collective-permute-done), channel_id=1, source_target_pairs={{0,32},{32,64},{64,96},{96,128},{128,160},{160,192},{192,224},{224... | collective-permute-start | bytes 196616 | tf_op jit(solution)/shard_map/ppermute | solution.py:48
  108.2 4.9 %collective-permute-start.2 = (bf16[256,128]{0,1:T(8,128)(2,1)S(1)}, bf16[256,128]{0,1:T(8,128)(2,1)S(1)}, u32[]{:S(2)}, u32[]{:S(2)}) collective-permute-start(bf16[256,128]{0,1:T(8,128)(2,1)S(1)} %collective-permute-done.1), channel_id=1, source_target_pairs={{0,32},{32,64},{64,96},{96,128},{128,160},{160,192},{192,224},{224... | collective-permute-start | bytes 196616 | tf_op jit(solution)/shard_map/ppermute | solution.py:48
  113.1 4.9 %collective-permute-start.3 = (bf16[256,128]{0,1:T(8,128)(2,1)S(1)}, bf16[256,128]{0,1:T(8,128)(2,1)S(1)}, u32[]{:S(2)}, u32[]{:S(2)}) collective-permute-start(bf16[256,128]{0,1:T(8,128)(2,1)S(1)} %collective-permute-done.2), channel_id=1, source_target_pairs={{0,32},{32,64},{64,96},{96,128},{128,160},{160,192},{192,224},{224... | collective-permute-start | bytes 196616 | tf_op jit(solution)/shard_map/ppermute | solution.py:48
  118.0 4.9 %collective-permute-start.4 = (bf16[256,128]{0,1:T(8,128)(2,1)S(1)}, bf16[256,128]{0,1:T(8,128)(2,1)S(1)}, u32[]{:S(2)}, u32[]{:S(2)}) collective-permute-start(bf16[256,128]{0,1:T(8,128)(2,1)S(1)} %collective-permute-done.3), channel_id=1, source_target_pairs={{0,32},{32,64},{64,96},{96,128},{128,160},{160,192},{192,224},{224... | collective-permute-start | bytes 196616 | tf_op jit(solution)/shard_map/ppermute | solution.py:48
  122.9 4.9 %collective-permute-start.5 = (bf16[256,128]{0,1:T(8,128)(2,1)S(1)}, bf16[256,128]{0,1:T(8,128)(2,1)S(1)}, u32[]{:S(2)}, u32[]{:S(2)}) collective-permute-start(bf16[256,128]{0,1:T(8,128)(2,1)S(1)} %collective-permute-done.4), channel_id=1, source_target_pairs={{0,32},{32,64},{64,96},{96,128},{128,160},{160,192},{192,224},{224... | collective-permute-start | bytes 196616 | tf_op jit(solution)/shard_map/ppermute | solution.py:48
  127.8 4.9 %collective-permute-start.6 = (bf16[256,128]{0,1:T(8,128)(2,1)S(1)}, bf16[256,128]{0,1:T(8,128)(2,1)S(1)}, u32[]{:S(2)}, u32[]{:S(2)}) collective-permute-start(bf16[256,128]{0,1:T(8,128)(2,1)S(1)} %collective-permute-done.5), channel_id=1, source_target_pairs={{0,32},{32,64},{64,96},{96,128},{128,160},{160,192},{192,224},{224... | collective-permute-start | bytes 196616 | tf_op jit(solution)/shard_map/ppermute | solution.py:48
  132.7 4.9 %collective-permute-start.7 = (bf16[256,128]{0,1:T(8,128)(2,1)S(1)}, bf16[256,128]{0,1:T(8,128)(2,1)S(1)}, u32[]{:S(2)}, u32[]{:S(2)}) collective-permute-start(bf16[256,128]{0,1:T(8,128)(2,1)S(1)} %collective-permute-done.6), channel_id=1, source_target_pairs={{0,32},{32,64},{64,96},{96,128},{128,160},{160,192},{192,224},{224... | collective-permute-start | bytes 196616 | tf_op jit(solution)/shard_map/ppermute | solution.py:48
  137.6 4.9 %collective-permute-start.8 = (bf16[256,128]{0,1:T(8,128)(2,1)S(1)}, bf16[256,128]{0,1:T(8,128)(2,1)S(1)}, u32[]{:S(2)}, u32[]{:S(2)}) collective-permute-start(bf16[256,128]{0,1:T(8,128)(2,1)S(1)} %collective-permute-done.7), channel_id=1, source_target_pairs={{0,32},{32,64},{64,96},{96,128},{128,160},{160,192},{192,224},{224... | collective-permute-start | bytes 196616 | tf_op jit(solution)/shard_map/ppermute | solution.py:48
  142.5 4.9 %collective-permute-start.9 = (bf16[256,128]{0,1:T(8,128)(2,1)S(1)}, bf16[256,128]{0,1:T(8,128)(2,1)S(1)}, u32[]{:S(2)}, u32[]{:S(2)}) collective-permute-start(bf16[256,128]{0,1:T(8,128)(2,1)S(1)} %collective-permute-done.8), channel_id=1, source_target_pairs={{0,32},{32,64},{64,96},{96,128},{128,160},{160,192},{192,224},{224... | collective-permute-start | bytes 196616 | tf_op jit(solution)/shard_map/ppermute | solution.py:48
  147.4 4.9 %collective-permute-start.10 = (bf16[256,128]{0,1:T(8,128)(2,1)S(1)}, bf16[256,128]{0,1:T(8,128)(2,1)S(1)}, u32[]{:S(2)}, u32[]{:S(2)}) collective-permute-start(bf16[256,128]{0,1:T(8,128)(2,1)S(1)} %collective-permute-done.9), channel_id=1, source_target_pairs={{0,32},{32,64},{64,96},{96,128},{128,160},{160,192},{192,224},{224... | collective-permute-start | bytes 196616 | tf_op jit(solution)/shard_map/ppermute | solution.py:48
  152.3 4.9 %collective-permute-start.11 = (bf16[256,128]{0,1:T(8,128)(2,1)S(1)}, bf16[256,128]{0,1:T(8,128)(2,1)S(1)}, u32[]{:S(2)}, u32[]{:S(2)}) collective-permute-start(bf16[256,128]{0,1:T(8,128)(2,1)S(1)} %collective-permute-done.10), channel_id=1, source_target_pairs={{0,32},{32,64},{64,96},{96,128},{128,160},{160,192},{192,224},{224... | collective-permute-start | bytes 196616 | tf_op jit(solution)/shard_map/ppermute | solution.py:48
  157.2 4.9 %collective-permute-start.12 = (bf16[256,128]{0,1:T(8,128)(2,1)S(1)}, bf16[256,128]{0,1:T(8,128)(2,1)S(1)}, u32[]{:S(2)}, u32[]{:S(2)}) collective-permute-start(bf16[256,128]{0,1:T(8,128)(2,1)S(1)} %collective-permute-done.11), channel_id=1, source_target_pairs={{0,32},{32,64},{64,96},{96,128},{128,160},{160,192},{192,224},{224... | collective-permute-start | bytes 196616 | tf_op jit(solution)/shard_map/ppermute | solution.py:48
  162.1 4.9 %collective-permute-start.13 = (bf16[256,128]{0,1:T(8,128)(2,1)S(1)}, bf16[256,128]{0,1:T(8,128)(2,1)S(1)}, u32[]{:S(2)}, u32[]{:S(2)}) collective-permute-start(bf16[256,128]{0,1:T(8,128)(2,1)S(1)} %collective-permute-done.12), channel_id=1, source_target_pairs={{0,32},{32,64},{64,96},{96,128},{128,160},{160,192},{192,224},{224... | collective-permute-start | bytes 196616 | tf_op jit(solution)/shard_map/ppermute | solution.py:48
  167.0 4.9 %collective-permute-start.14 = (bf16[256,128]{0,1:T(8,128)(2,1)S(1)}, bf16[256,128]{0,1:T(8,128)(2,1)S(1)}, u32[]{:S(2)}, u32[]{:S(2)}) collective-permute-start(bf16[256,128]{0,1:T(8,128)(2,1)S(1)} %collective-permute-done.13), channel_id=1, source_target_pairs={{0,32},{32,64},{64,96},{96,128},{128,160},{160,192},{192,224},{224... | collective-permute-start | bytes 196616 | tf_op jit(solution)/shard_map/ppermute | solution.py:48
  174.6 11.8 %copy-start.2 = (f32[128]{0:T(128)S(1)}, f32[128]{0:T(128)}, u32[]{:S(2)}) copy-start(f32[128]{0:T(128)} %param.12) | copy-start | bytes 1540
Sparse Core Ops, SparseCore 0:
  10.4 83.9 all-gather.2
  187.2 243.5 all-gather.4
